TPU v7x, 768 devices: a whole 4x8x12 slice. The times are simulated.
768 devices in a mesh: grp: 12 (over z), dom: 64 (over x, y, core).
Axes of the slice: x: 4, y: 8, z: 12, core: 2. Of those that a mesh axis runs over, the one named last changes fastest.
Arguments:
- cotangent: bfloat16 [884736, 256], P(('grp', 'dom')), as said below
- features: bfloat16 [393216, 256], P(('grp', 'dom')), may hold values from -6 to 6
- aggregated: bfloat16 [393216, 256], P(('grp', 'dom')), may hold values from -6 to 6
- w_self: bfloat16 [256, 256], replicated, may hold values from -0.375 to 0.375
- w_neigh: bfloat16 [256, 256], replicated, may hold values from -0.375 to 0.375
- edge_tiles: bfloat16 [49152, 128, 128], P(('grp', 'dom')), may hold values from -0.1875 to 0.1875
- tile_rows: int32 [49152], P(('grp', 'dom')), may hold values from 0 to 8
- tile_cols: int32 [49152], P(('grp', 'dom')), may hold values from 0 to 8
- mirror_rows: int32 [768, 64, 8], P(('grp', 'dom')), may hold values from 0 to 511, as said below
- mirror_count: int32 [768, 64], P(('grp', 'dom')), may hold values from 0 to 8
- cross_rows: int32 [768, 12, 4], P(('grp', 'dom')), may hold values from 0 to 511, as said below
- cross_count: int32 [768, 12], P(('grp', 'dom')), may hold values from 0 to 4
Outputs:
- grad_slots: bfloat16 [884736, 256], P(('grp', 'dom'))
- grad_weights: float32 [2, 256, 256], replicated
Inputs may be any that keep to these rules, and one draw needn't show every extreme that they name: Mirror slots of cotangent hold the row of their master when live, zeros when dead; empty slots are zero. `mirror_rows`: entries of one list are distinct; only the first mirror_count entries are live. `cross_rows`: entries of one list are distinct; only the first cross_count entries are live.
All inputs are finite; a program needn't handle non-finite values.
Results may differ from a plain program's by a relative error of at most 0.0042.
Values may be sent and summed in bfloat16 or wider, within the bound.
A program may use at most 32 MiB of HBM per device.

v0:
```python
import math

import jax
import jax.numpy as jnp
from jax import lax
from jax.sharding import PartitionSpec as P


def times_transpose(left, weight):
    return lax.dot_general(
        left, weight, (((1,), (1,)), ((), ())), preferred_element_type=jnp.float32
    )


def body(
    cotangent,
    features,
    aggregated,
    w_self,
    w_neigh,
    edge_tiles,
    tile_rows,
    tile_cols,
    mirror_rows,
    mirror_count,
    cross_rows,
    cross_count,
):
    domain_size = lax.axis_size("dom")
    group_total = lax.axis_size("grp")
    slot_count, feature_width = cotangent.shape
    masters = features.shape[0]
    tile_size = edge_tiles.shape[1]
    blocks = slot_count // tile_size
    tile_total = edge_tiles.shape[0]
    batch_tiles = math.gcd(tile_total, 32)
    batch_count = tile_total // batch_tiles
    capacity = mirror_rows.shape[2]
    cross_capacity = cross_rows.shape[2]
    inner_end = masters + domain_size * capacity
    outer_end = inner_end + group_total * cross_capacity
    neighbor_grad = times_transpose(cotangent, w_neigh).astype(jnp.bfloat16)
    grad_blocks = neighbor_grad.reshape(blocks, tile_size, feature_width)
    block_ids = jnp.arange(blocks, dtype=jnp.int32)

    def tile_step(running, inputs):
        tile_values, rows_in, cols_in = inputs
        taken_blocks = jnp.take(grad_blocks, rows_in, axis=0)
        product = jnp.einsum(
            "kij,kif->kjf", tile_values, taken_blocks, preferred_element_type=jnp.float32
        )
        selector = (cols_in[:, None] == block_ids[None, :]).astype(jnp.float32)
        added = jnp.einsum("kc,kjf->cjf", selector, product, precision=lax.Precision.HIGHEST)
        return (running + added, None)

    start_sum = jnp.zeros((blocks, tile_size, feature_width), jnp.float32)
    partial_sum, _ = lax.scan(
        tile_step,
        start_sum,
        (
            edge_tiles.reshape(batch_count, batch_tiles, tile_size, tile_size),
            tile_rows.reshape(batch_count, batch_tiles),
            tile_cols.reshape(batch_count, batch_tiles),
        ),
    )
    partial_sum = partial_sum.reshape(slot_count, feature_width)
    master_cot = cotangent[:masters]
    own_term = times_transpose(master_cot, w_self) + partial_sum[:masters]
    inner_sums = partial_sum[masters:inner_end].reshape(domain_size, capacity, feature_width)
    outer_sums = partial_sum[inner_end:outer_end].reshape(
        group_total, cross_capacity, feature_width
    )
    inner_back = lax.all_to_all(inner_sums, "dom", split_axis=0, concat_axis=0, tiled=True)
    outer_back = lax.all_to_all(
        outer_sums.astype(jnp.bfloat16), "grp", split_axis=0, concat_axis=0, tiled=True
    ).astype(outer_sums.dtype)
    inner_live = jnp.arange(capacity, dtype=jnp.int32)[None, :] < mirror_count[0][:, None]
    outer_live = jnp.arange(cross_capacity, dtype=jnp.int32)[None, :] < cross_count[0][:, None]
    inner_back = jnp.where(inner_live[:, :, None], inner_back, jnp.zeros((), jnp.float32))
    outer_back = jnp.where(outer_live[:, :, None], outer_back, jnp.zeros((), jnp.float32))
    totals = own_term.at[mirror_rows[0].reshape(-1)].add(inner_back.reshape(-1, feature_width))
    totals = totals.at[cross_rows[0].reshape(-1)].add(outer_back.reshape(-1, feature_width))
    grad_master = totals.astype(jnp.bfloat16)
    inner_send = jnp.where(
        inner_live[:, :, None],
        jnp.take(grad_master, mirror_rows[0], axis=0),
        jnp.zeros((), jnp.bfloat16),
    )
    outer_send = jnp.where(
        outer_live[:, :, None],
        jnp.take(grad_master, cross_rows[0], axis=0),
        jnp.zeros((), jnp.bfloat16),
    )
    inner_copy = lax.all_to_all(inner_send, "dom", split_axis=0, concat_axis=0, tiled=True)
    outer_copy = lax.all_to_all(outer_send, "grp", split_axis=0, concat_axis=0, tiled=True)
    padding = jnp.zeros((slot_count - outer_end, feature_width), jnp.bfloat16)
    grad_slots = jnp.concatenate(
        [
            grad_master,
            inner_copy.reshape(-1, feature_width),
            outer_copy.reshape(-1, feature_width),
            padding,
        ],
        axis=0,
    )
    joined = jnp.concatenate([features, aggregated], axis=1)
    grad_scale = 1.0 / math.sqrt(masters * domain_size * group_total)
    local_term = lax.dot_general(
        joined, master_cot, (((0,), (0,)), ((), ())), preferred_element_type=jnp.float32
    )
    summed = lax.psum(local_term, ("grp", "dom"))
    grad_weights = (summed * grad_scale).reshape(2, feature_width, feature_width)
    return (grad_slots, grad_weights)


def solution(mesh):
    placed = (
        P(("grp", "dom"), None),
        P(("grp", "dom"), None),
        P(("grp", "dom"), None),
        P(),
        P(),
        P(("grp", "dom"), None, None),
        P(("grp", "dom")),
        P(("grp", "dom")),
        P(("grp", "dom"), None, None),
        P(("grp", "dom"), None),
        P(("grp", "dom"), None, None),
        P(("grp", "dom"), None),
    )
    return jax.shard_map(
        body, mesh=mesh, in_specs=placed, out_specs=(P(("grp", "dom"), None), P()), check_vma=False
    )
```

profile of v0, /device:TPU:1, one launch (start us, length us, event | category | flops | bytes accessed | tf_op | source)
XLA Modules:
  0.0 592.3 jit_solution(16874152566624953454)
XLA Ops:
  7.2 0.8 reshape.252
  8.0 0.7 reshape.254
  8.7 1.4 convolution_convert_fusion
  10.1 24.7 %while.11 = (s32[]{:T(128)}, f32[9,128,256]{2,0,1:T(8,128)}, s32[2,32]{1,0:T(2,128)S(1)}, bf16[2,32,128,128]{3,2,1,0:T(8,128)(2,1)}, s32[2,32]{1,0:T(2,128)S(1)}...) while((s32[]{:T(128)}, f32[9,128,256]{2,0,1:T(8,128)}, s32[2,32]{1,0:T(2,128)S(1)}, ...), condition=%wide.region_1.2_spmd.clone, body=%wide.region_0.1_spmd.clone.sunk | while | flops 383321664 | bytes 18093740 | solution.py:57
  10.1 0.7 gather_fusion
  10.9 4.0 fusion.49
  14.8 7.3 %select_add_fusion.2 = f32[9,128,256]{2,0,1:T(8,128)} fusion(f32[9,128,256]{2,0,1:T(8,128)} %get-tuple-element.123, f32[32,128,256]{2,1,0:T(8,128)} %fusion.49, pred[]{:T(512)S(6)} %compare.3, s32[32]{0:T(128)S(1)} %fusion.50), kind=kOutput, calls=%fused_computation.8.clone.1 | convolution fusion | flops 113836320 | bytes 6553729 | tf_op jit(solution)/shard_map/while/body/eval_jaxpr/kc,kjf->cjf/dot_general | solution.py:53
  22.1 0.7 gather_fusion
  22.9 4.0 fusion.49
  26.8 8.0 %select_add_fusion.2 = f32[9,128,256]{2,0,1:T(8,128)} fusion(f32[9,128,256]{2,0,1:T(8,128)} %get-tuple-element.123, f32[32,128,256]{2,1,0:T(8,128)} %fusion.49, pred[]{:T(512)S(6)} %compare.3, s32[32]{0:T(128)S(1)} %fusion.50), kind=kOutput, calls=%fused_computation.8.clone.1 | convolution fusion | flops 113836320 | bytes 6553729 | tf_op jit(solution)/shard_map/while/body/eval_jaxpr/kc,kjf->cjf/dot_general | solution.py:53
  34.8 2.3 fusion.33
  37.2 0.6 convert_element_type.15
  37.8 15.7 %all-to-all-start.1 = ((bf16[12,4,256]{2,1,0:T(4,128)(2,1)}), bf16[12,4,256]{2,1,0:T(4,128)(2,1)S(1)}, u32[]{:S(2)}, u32[]{:S(2)}) async-start(bf16[12,4,256]{2,1,0:T(4,128)(2,1)} %convert_element_type.15), calls=%async_computation.1 | async-start | bytes 49152 | tf_op jit(solution)/shard_map/all_to_all | solution.py:74
  53.5 1.4 slice.18
  55.1 0.8 slice.28
  56.9 5.9 all-to-all-done.1
  62.8 12.2 %all-to-all-start = ((f32[64,8,256]{2,1,0:T(8,128)}), f32[64,8,256]{2,1,0:T(8,128)S(1)}, u32[]{:S(2)}, u32[]{:S(2)}) async-start(f32[64,8,256]{2,1,0:T(8,128)} %bitcast.5), calls=%async_computation | async-start | bytes 1048576 | tf_op jit(solution)/shard_map/all_to_all | solution.py:73
  75.1 0.3 convolution_add_fusion
  75.5 16.8 %all-to-all-done = f32[64,8,256]{2,1,0:T(8,128)S(1)} async-done(((f32[64,8,256]{2,1,0:T(8,128)}), f32[64,8,256]{2,1,0:T(8,128)S(1)}, u32[]{:S(2)}, u32[]{:S(2)}) %all-to-all-start) | async-done | bytes 524320 | tf_op jit(solution)/shard_map/all_to_all | solution.py:73
  92.3 3.7 scatter_custom_fusion
  96.0 1.1 scatter_fusion
  97.1 2.0 gather_fusion.1
  99.1 0.7 gather_fusion.2
  99.8 0.7 select_select_fusion
  100.5 3.5 all-to-all-start.3
  104.0 0.9 fusion.26
  104.9 8.3 %all-to-all-done.3 = bf16[12,4,256]{2,1,0:T(4,128)(2,1)S(1)} async-done(((bf16[12,4,256]{2,1,0:T(4,128)(2,1)}), bf16[12,4,256]{2,1,0:T(4,128)(2,1)S(1)}, u32[]{:S(2)}, u32[]{:S(2)}) %all-to-all-start.3) | async-done | bytes 24608 | tf_op jit(solution)/shard_map/all_to_all | solution.py:95
  113.2 7.4 %all-to-all-start.2 = ((bf16[64,8,256]{2,1,0:T(8,128)(2,1)}), bf16[64,8,256]{2,1,0:T(8,128)(2,1)S(1)}, u32[]{:S(2)}, u32[]{:S(2)}) async-start(bf16[64,8,256]{2,1,0:T(8,128)(2,1)} %fusion.26), calls=%async_computation.2 | async-start | bytes 524288 | tf_op jit(solution)/shard_map/all_to_all | solution.py:94
  120.7 1.1 fusion.19
  122.0 460.6 %all-reduce.2.cloned.1.call-done = f32[512,256]{1,0:T(8,128)} async-done(((f32[512,256]{1,0:T(8,128)}), f32[512,256]{1,0:T(8,128)}) %all-reduce.2.cloned.1.call-update) | async-done | bytes 524304 | tf_op jit(solution)/shard_map/psum | solution.py:111
  582.6 1.9 broadcast_multiply_fusion
  584.5 1.0 maximum_maximum_fusion
  (59 shorter events, 1.6 us)
Async XLA Ops:
  7.2 1.5 copy-start
  34.8 20.1 %copy-start.3 = (s32[1,64,8]{1,2,0:T(8,128)S(1)}, s32[1,64,8]{1,2,0:T(8,128)}, u32[]{:S(2)}) copy-start(s32[1,64,8]{1,2,0:T(8,128)} %param.22) | copy-start | bytes 6148
  34.8 20.2 %copy-start.4 = (s32[1,12,4]{1,2,0:T(4,128)S(1)}, s32[1,12,4]{1,2,0:T(4,128)}, u32[]{:S(2)}) copy-start(s32[1,12,4]{1,2,0:T(4,128)} %param.24) | copy-start | bytes 580
  37.1 19.0 %copy-start.5 = (s32[1,12]{1,0:T(1,128)S(1)}, s32[1,12]{1,0:T(1,128)}, u32[]{:S(2)}) copy-start(s32[1,12]{1,0:T(1,128)} %param.25) | copy-start | bytes 148
  37.8 25.0 %all-to-all-start.1 = ((bf16[12,4,256]{2,1,0:T(4,128)(2,1)}), bf16[12,4,256]{2,1,0:T(4,128)(2,1)S(1)}, u32[]{:S(2)}, u32[]{:S(2)}) async-start(bf16[12,4,256]{2,1,0:T(4,128)(2,1)} %convert_element_type.15), calls=%async_computation.1 | async-start | bytes 49152 | tf_op jit(solution)/shard_map/all_to_all | solution.py:74
  53.5 21.5 %copy-start.6 = (s32[1,64]{1,0:T(1,128)S(1)}, s32[1,64]{1,0:T(1,128)}, u32[]{:S(2)}) copy-start(s32[1,64]{1,0:T(1,128)} %param.23) | copy-start | bytes 772
  53.5 21.6 %copy-start.1 = (bf16[1152,256]{1,0:T(8,128)(2,1)S(1)}, bf16[1152,256]{1,0:T(8,128)(2,1)}, u32[]{:S(2)}) copy-start(bf16[1152,256]{1,0:T(8,128)(2,1)} %param.14) | copy-start | bytes 1769476
  53.5 21.6 %copy-start.2 = (bf16[256,256]{1,0:T(8,128)(2,1)S(1)}, bf16[256,256]{1,0:T(8,128)(2,1)}, u32[]{:S(2)}) copy-start(bf16[256,256]{1,0:T(8,128)(2,1)} %param.17) | copy-start | bytes 393220
  62.8 29.5 %all-to-all-start = ((f32[64,8,256]{2,1,0:T(8,128)}), f32[64,8,256]{2,1,0:T(8,128)S(1)}, u32[]{:S(2)}, u32[]{:S(2)}) async-start(f32[64,8,256]{2,1,0:T(8,128)} %bitcast.5), calls=%async_computation | async-start | bytes 1048576 | tf_op jit(solution)/shard_map/all_to_all | solution.py:73
  97.1 23.6 %copy-start.7 = (bf16[512,256]{1,0:T(8,128)(2,1)S(1)}, bf16[512,256]{1,0:T(8,128)(2,1)}, u32[]{:S(2)}) copy-start(bf16[512,256]{1,0:T(8,128)(2,1)} %param.16) | copy-start | bytes 786436
  97.1 23.6 %copy-start.8 = (bf16[512,256]{1,0:T(8,128)(2,1)S(1)}, bf16[512,256]{1,0:T(8,128)(2,1)}, u32[]{:S(2)}) copy-start(bf16[512,256]{1,0:T(8,128)(2,1)} %param.15) | copy-start | bytes 786436
  100.5 12.7 %all-to-all-start.3 = ((bf16[12,4,256]{2,1,0:T(4,128)(2,1)}), bf16[12,4,256]{2,1,0:T(4,128)(2,1)S(1)}, u32[]{:S(2)}, u32[]{:S(2)}) async-start(bf16[12,4,256]{2,1,0:T(4,128)(2,1)} %select_select_fusion), calls=%async_computation.3 | async-start | bytes 49152 | tf_op jit(solution)/shard_map/all_to_all | solution.py:95
  113.2 471.3 %all-to-all-start.2 = ((bf16[64,8,256]{2,1,0:T(8,128)(2,1)}), bf16[64,8,256]{2,1,0:T(8,128)(2,1)S(1)}, u32[]{:S(2)}, u32[]{:S(2)}) async-start(bf16[64,8,256]{2,1,0:T(8,128)(2,1)} %fusion.26), calls=%async_computation.2 | async-start | bytes 524288 | tf_op jit(solution)/shard_map/all_to_all | solution.py:94
  120.6 461.9 %all-reduce.2.cloned.1.call-start = ((), (), s32[]{:S(2)}) async-start(), calls=%async_computation.4 | async-start | bytes 1048576 | tf_op jit(solution)/shard_map/psum | solution.py:111
Sparse Core Ops, SparseCore 0:
  127.4 455.0 all-reduce.1
where the time goes:
time: 593 us; the launch traced here: 592 us
  waiting for transfers between devices  492 us (83%)
  starting transfers between devices  38.9 us (7%)
  matrix products  26 us (4%)
  between operations  14.3 us (2%)
  other arithmetic  12 us (2%)
  local copies, waits for them, and re-layouts  9.52 us (2%)
    psum x1, waiting for transfers between devices, body(): summed = lax.psum(local_term, ('grp', 'dom'))  461 us
    all_to_all x1, waiting for transfers between devices, body(): lax.all_to_all(inner_sums, 'dom', split_axis=0, concat_axis=0, tiled=True)  16.8 us
    all_to_all x1, starting transfers between devices, body(): lax.all_to_all(outer_sums.astype(jnp.bfloat16), 'grp', split_axis=0, conc...  15.7 us
    dot_general x2, matrix products, tile_step(): jnp.einsum('kc,kjf->cjf', selector, product, precision=lax.Precision.HIGH...  15.3 us
    all_to_all x1, starting transfers between devices, body(): lax.all_to_all(inner_sums, 'dom', split_axis=0, concat_axis=0, tiled=True)  12.2 us
  transfers between devices with their start and end apart: 5, of which 4 were waited for; matrix products, arithmetic and copies ran while one was open for 1% of the time, Pallas kernels for 0%

commit v1 on v0

v1 whole, which is shorter than its diff:
```python
import functools
import math

import jax
import jax.numpy as jnp
from jax import lax
from jax.experimental import pallas as pl
from jax.experimental.pallas import tpu as pltpu
from jax.sharding import PartitionSpec as P

F32 = jnp.float32
BF16 = jnp.bfloat16
MESH = pl.DeviceIdType.MESH
UNROLL = 8


def dot_tt(left, right):
    return lax.dot_general(left, right, (((1,), (1,)), ((), ())), preferred_element_type=F32)


def dot_nn(left, right):
    return lax.dot_general(left, right, (((1,), (0,)), ((), ())), preferred_element_type=F32)


def dot_tn(left, right):
    return lax.dot_general(left, right, (((0,), (0,)), ((), ())), preferred_element_type=F32)


def iota(shape, axis):
    return lax.broadcasted_iota(jnp.int32, shape, axis)


def one_hot(mask):
    return jnp.where(mask, 1.0, 0.0).astype(F32)


def list_lanes(rows_ref, count_ref, lanes):
    peers, capacity = rows_ref.shape[1], rows_ref.shape[2]
    entry = iota((capacity, lanes), 1) % 8
    pick = one_hot(entry == iota((capacity, lanes), 0))
    spread = lax.dot_general(
        rows_ref[0].astype(F32), pick, (((1,), (0,)), ((), ())),
        precision=lax.Precision.HIGHEST, preferred_element_type=F32,
    )
    mine = iota((peers, lanes), 1) // 8 == iota((peers, lanes), 0)
    rows = jnp.sum(jnp.where(mine, spread, 0.0), axis=0, keepdims=True)
    counts = lax.dot_general(
        count_ref[...].astype(F32), one_hot(mine), (((1,), (0,)), ((), ())),
        precision=lax.Precision.HIGHEST, preferred_element_type=F32,
    )
    live = (iota((1, lanes), 1) % 8).astype(F32) < counts
    return jnp.where(live, rows, -1.0)


def to_chunks(rows):
    count, half = rows.shape[0] // 8, rows.shape[1] // 2
    left = rows[:, :half].reshape(count, 8, half)
    right = rows[:, half:].reshape(count, 8, half)
    return jnp.concatenate([left, right], axis=1).astype(BF16)


def from_chunks(chunks):
    count, half = chunks.shape[0], chunks.shape[2]
    wide = chunks.astype(F32)
    left = wide[:, :8].reshape(count * 8, half)
    right = wide[:, 8:].reshape(count * 8, half)
    return jnp.concatenate([left, right], axis=1).astype(BF16)


def kernel(
    sizes, scale,
    cot_hbm, feat_hbm, agg_hbm, wself_hbm, wneigh_hbm, tiles_hbm,
    trow, tcol, mrow, mcnt, xrow, xcnt,
    slots_out, weights_out,
    cot, feat, agg, wself, wneigh, tiles, grads, run, part, own,
    pick, pick_t, send_a, recv_a, send_b, recv_b,
    sendx_a, recvx_a, sendx_b, recvx_b,
    w_local, w_pair, w_x, w_xin, w_z, w_zin, w_yin, w_zall, w_xall, w_other,
    load_sem, ex_sem, w_send, w_recv,
):
    nx, ny, nz, granules = sizes
    nd = nx * ny * 2
    masters = feat.shape[0]
    blocks = grads.shape[0]
    tile_total = tiles.shape[0]
    inner_end = masters + nd * 8
    z = lax.axis_index("grp")
    d = lax.axis_index("dom")
    core = d % 2
    y = (d // 2) % ny
    x = d // (2 * ny)

    def dom_of(xx, yy, cc):
        return (xx * ny + yy) * 2 + cc

    def hop(offset):
        return dom_of(
            (x + offset // (2 * ny)) % nx, (y + (offset // 2) % ny) % ny, (core + offset) % 2
        )

    loads = []
    for place, (src, dst) in enumerate(
        [(cot_hbm, cot), (feat_hbm, feat), (agg_hbm, agg), (wneigh_hbm, wneigh),
         (tiles_hbm, tiles), (wself_hbm, wself)]
    ):
        load = pltpu.make_async_copy(src, dst, load_sem.at[place])
        load.start()
        loads.append(load)

    barrier = pltpu.get_barrier_semaphore()

    @pl.loop(1, nd)
    def _(offset):
        pl.semaphore_signal(barrier, inc=1, device_id=(z, hop(offset)), device_id_type=MESH)

    @pl.loop(1, nz)
    def _(offset):
        pl.semaphore_signal(
            barrier, inc=1, device_id=((z + offset) % nz, d), device_id_type=MESH
        )

    def push(src, dst, stage, target):
        copy = pltpu.make_async_remote_copy(
            src_ref=src, dst_ref=dst, send_sem=w_send.at[stage], recv_sem=w_recv.at[stage],
            device_id=target, device_id_type=MESH,
        )
        copy.start()

    def settle(ref, sem):
        pltpu.make_async_copy(ref, ref, sem).wait()

    loads[0].wait()
    loads[1].wait()
    w_local[0] = dot_tn(feat[...], cot[:masters])
    loads[2].wait()
    w_local[1] = dot_tn(agg[...], cot[:masters])

    loads[3].wait()
    for block in range(blocks):
        rows = slice(block * 128, block * 128 + 128)
        grads[block] = dot_tt(cot[rows], wneigh[...]).astype(BF16)

    pl.semaphore_wait(barrier, nd - 1 + nz - 1)
    partner = (z, d + 1 - 2 * core)
    push(w_local.at[1 - core], w_pair, 0, partner)

    run[0] = jnp.zeros(run.shape[1:], F32)
    loads[4].wait()

    def tile_group(group, last):
        for step in range(UNROLL):
            k = group * UNROLL + step
            column = tcol[k]
            before = last[0]
            for block in range(1, blocks):
                before = jnp.where(column == block, last[block], before)
            product = dot_tn(tiles[k], grads[trow[k]])
            run[k + 1] = product + run[before]
            last = tuple(
                jnp.where(column == block, k + 1, last[block]) for block in range(blocks)
            )
        return last

    last = lax.fori_loop(
        0, tile_total // UNROLL, tile_group, tuple(jnp.int32(0) for _ in range(blocks))
    )
    for block in range(blocks):
        part[block * 128:block * 128 + 128] = run[last[block]]

    send_a[...] = to_chunks(part[masters:inner_end])
    spread = (iota((128, 128), 0) // 8 == iota((128, 128), 1) // 4) & (
        iota((128, 128), 0) % 8 == iota((128, 128), 1) % 4
    ) & (iota((128, 128), 1) < nz * 4)
    sendx_a[...] = to_chunks(
        dot_nn(one_hot(spread).astype(BF16), part[inner_end:inner_end + 128].astype(BF16))
    )

    def exchange(send, recv, sendx, recvx, stage):
        @pl.loop(1, nz)
        def _(offset):
            target = (z + offset) % nz
            pltpu.make_async_remote_copy(
                src_ref=sendx.at[target], dst_ref=recvx.at[z],
                send_sem=ex_sem.at[stage], recv_sem=ex_sem.at[stage + 1],
                device_id=(target, d), device_id_type=MESH,
            ).start()

        @pl.loop(1, nd)
        def _(offset):
            target = hop(offset)
            pltpu.make_async_remote_copy(
                src_ref=send.at[target], dst_ref=recv.at[d],
                send_sem=ex_sem.at[stage + 2], recv_sem=ex_sem.at[stage + 3],
                device_id=(z, target), device_id_type=MESH,
            ).start()

        recv[d] = send[d]
        recvx[z] = sendx[z]
        for slot in range(nz, recvx.shape[0]):
            recvx[slot] = jnp.zeros(recvx.shape[1:], BF16)

    def arrived(recv, recvx, stage):
        settle(recvx.at[pl.ds(0, nz - 1)], ex_sem.at[stage + 1])
        settle(recv.at[pl.ds(0, nd - 1)], ex_sem.at[stage + 3])

    def sent(send, sendx, stage):
        settle(sendx.at[pl.ds(0, nz - 1)], ex_sem.at[stage])
        settle(send.at[pl.ds(0, nd - 1)], ex_sem.at[stage + 2])

    exchange(send_a, recv_a, sendx_a, recvx_a, 0)

    settle(w_pair, w_recv.at[0])
    w_x[...] = (w_local[core] + w_pair[...]).reshape(w_x.shape)
    for step in range(1, nx):
        to_x = (x + step) % nx
        push(w_x.at[to_x], w_xin.at[step - 1], 1, (z, dom_of(to_x, y, core)))

    loads[5].wait()
    own[...] = dot_tt(cot[:masters], wself[...]) + part[:masters]
    inner_lanes = pick.shape[1] - 128
    lanes = jnp.concatenate(
        [list_lanes(mrow, mcnt, inner_lanes), list_lanes(xrow, xcnt, 128)], axis=1
    )
    master_of = iota(pick.shape, 0).astype(F32)
    pick[...] = one_hot(master_of == lanes).astype(BF16)

    settle(w_xin, w_recv.at[1])
    share = w_x[x]
    for step in range(nx - 1):
        share = share + w_xin[step]
    w_z[...] = share.reshape(w_z.shape)

    def owner_of(granule):
        return (granule * nz) // granules

    mine = (z * granules + nz - 1) // nz
    owner = owner_of(mine) == z

    @pl.loop(0, granules)
    def _(granule):
        target = owner_of(granule)

        @pl.when(target != z)
        def _():
            push(w_z.at[granule], w_zin.at[z], 2, (target, d))

    slots_t = jnp.transpose(jnp.broadcast_to(lanes, (128, lanes.shape[1])))
    for block in range(masters // 128):
        columns = slice(block * 128, block * 128 + 128)
        master_at = (iota(slots_t.shape, 1) + block * 128).astype(F32)
        pick_t[:, columns] = one_hot(slots_t == master_at).astype(BF16)

    @pl.when(owner)
    def _():
        w_zin[z] = w_z[mine]
        settle(w_zin.at[pl.ds(0, nz - 1)], w_recv.at[2])
        total = w_zin[0]
        for step in range(1, nz):
            total = total + w_zin[step]
        w_yin[y] = total

        @pl.loop(1, ny)
        def _(step):
            push(w_yin.at[y], w_yin.at[y], 3, (z, dom_of(x, (y + step) % ny, core)))

    arrived(recv_a, recvx_a, 0)
    back = jnp.concatenate([from_chunks(recv_a[...]), from_chunks(recvx_a[...])], axis=0)
    master = (own[...] + dot_nn(pick[...], back)).astype(BF16)
    slots_out[:masters] = master
    copies = dot_nn(pick_t[...], master)
    send_b[...] = to_chunks(copies[:inner_lanes])
    sendx_b[...] = to_chunks(copies[inner_lanes:])
    exchange(send_b, recv_b, sendx_b, recvx_b, 4)

    @pl.when(owner)
    def _():
        settle(w_yin.at[pl.ds(0, ny - 1)], w_recv.at[3])
        total = w_yin[0]
        for step in range(1, ny):
            total = total + w_yin[step]
        w_zall[mine] = total * scale

        @pl.loop(1, nz)
        def _(step):
            push(w_zall.at[mine], w_zall.at[mine], 4, ((z + step) % nz, d))

        settle(w_zall.at[pl.ds(0, granules - 1)], w_recv.at[4])

    @pl.when(jnp.logical_not(owner))
    def _():
        settle(w_zall, w_recv.at[4])

    w_xall[x] = w_zall[...].reshape(w_xall.shape[1:])
    for step in range(1, nx):
        push(w_xall.at[x], w_xall.at[x], 5, (z, dom_of((x + step) % nx, y, core)))
    settle(w_xall.at[pl.ds(0, nx - 1)], w_recv.at[5])
    push(w_xall, w_other, 6, partner)
    weights_out[core] = w_xall[...].reshape(weights_out.shape[1:])

    arrived(recv_b, recvx_b, 4)
    slots_out[masters:inner_end] = from_chunks(recv_b[...])
    gather = (iota((128, 128), 1) // 8 == iota((128, 128), 0) // 4) & (
        iota((128, 128), 1) % 8 == iota((128, 128), 0) % 4
    ) & (iota((128, 128), 0) < nz * 4)
    slots_out[inner_end:inner_end + 128] = dot_nn(
        one_hot(gather).astype(BF16), from_chunks(recvx_b[...])
    ).astype(BF16)
    tail = slots_out.shape[0] - inner_end - 128
    if tail:
        slots_out[inner_end + 128:] = jnp.zeros((tail, slots_out.shape[1]), BF16)

    settle(w_other, w_recv.at[6])
    weights_out[1 - core] = w_other[...].reshape(weights_out.shape[1:])

    sent(send_a, sendx_a, 0)
    sent(send_b, sendx_b, 4)
    settle(w_pair, w_send.at[0])
    settle(w_xin, w_send.at[1])

    @pl.when(owner)
    def _():
        settle(w_z.at[pl.ds(0, granules - 1)], w_send.at[2])
        settle(w_yin.at[pl.ds(0, ny - 1)], w_send.at[3])
        settle(w_zin.at[pl.ds(0, nz - 1)], w_send.at[4])

    @pl.when(jnp.logical_not(owner))
    def _():
        settle(w_z, w_send.at[2])

    settle(w_xall.at[pl.ds(0, nx - 1)], w_send.at[5])
    settle(w_other, w_send.at[6])


def body(
    sizes,
    cotangent, features, aggregated, w_self, w_neigh, edge_tiles,
    tile_rows, tile_cols, mirror_rows, mirror_count, cross_rows, cross_count,
):
    nx, ny, nz, granules = sizes
    nd = nx * ny * 2
    slot_count, width = cotangent.shape
    masters = features.shape[0]
    tile_total = edge_tiles.shape[0]
    blocks = slot_count // 128
    scale = 1.0 / math.sqrt(masters * nd * nz)
    share = width // nx
    grain = share // granules
    any_spec = pl.BlockSpec(memory_space=pl.ANY)
    vmem = pl.BlockSpec(memory_space=pltpu.VMEM)
    smem = pl.BlockSpec(memory_space=pltpu.SMEM)
    lanes = (nd * 8 + 127) // 128 * 128 + 128
    chunk = (16, width // 2)
    dma = pltpu.SemaphoreType.DMA
    return pl.pallas_call(
        functools.partial(kernel, sizes, scale),
        out_shape=(
            jax.ShapeDtypeStruct((slot_count, width), BF16),
            jax.ShapeDtypeStruct((2, width, width), F32),
        ),
        in_specs=[any_spec] * 6 + [smem] * 2 + [vmem] * 4,
        out_specs=(vmem, vmem),
        scratch_shapes=[
            pltpu.VMEM(cotangent.shape, BF16),
            pltpu.VMEM(features.shape, BF16),
            pltpu.VMEM(aggregated.shape, BF16),
            pltpu.VMEM(w_self.shape, BF16),
            pltpu.VMEM(w_neigh.shape, BF16),
            pltpu.VMEM(edge_tiles.shape, BF16),
            pltpu.VMEM((blocks, 128, width), BF16),
            pltpu.VMEM((tile_total + 1, 128, width), F32),
            pltpu.VMEM((slot_count, width), F32),
            pltpu.VMEM((masters, width), F32),
            pltpu.VMEM((masters, lanes), BF16),
            pltpu.VMEM((lanes, masters), BF16),
            pltpu.VMEM((nd,) + chunk, BF16),
            pltpu.VMEM((nd,) + chunk, BF16),
            pltpu.VMEM((nd,) + chunk, BF16),
            pltpu.VMEM((nd,) + chunk, BF16),
            pltpu.VMEM((16,) + chunk, BF16),
            pltpu.VMEM((16,) + chunk, BF16),
            pltpu.VMEM((16,) + chunk, BF16),
            pltpu.VMEM((16,) + chunk, BF16),
            pltpu.VMEM((2, width, width), F32),
            pltpu.VMEM((width, width), F32),
            pltpu.VMEM((nx, share, width), F32),
            pltpu.VMEM((nx - 1, share, width), F32),
            pltpu.VMEM((granules, grain, width), F32),
            pltpu.VMEM((nz, grain, width), F32),
            pltpu.VMEM((ny, grain, width), F32),
            pltpu.VMEM((granules, grain, width), F32),
            pltpu.VMEM((nx, share, width), F32),
            pltpu.VMEM((nx, share, width), F32),
            dma((6,)),
            dma((8,)),
            dma((7,)),
            dma((7,)),
        ],
        compiler_params=pltpu.CompilerParams(
            collective_id=0, has_side_effects=True, vmem_limit_bytes=48 * 1024 * 1024
        ),
    )(
        cotangent, features, aggregated, w_self, w_neigh, edge_tiles,
        tile_rows, tile_cols, mirror_rows, mirror_count, cross_rows, cross_count,
    )


def solution(mesh, grid=(4, 8)):
    nx, ny = grid
    nz = mesh.shape["grp"]
    granules = 1
    while granules * 2 <= min(nz, 256 // nx // 8):
        granules *= 2
    both = ("grp", "dom")
    placed = (
        P(both, None), P(both, None), P(both, None), P(), P(), P(both, None, None),
        P(both), P(both), P(both, None, None), P(both, None), P(both, None, None),
        P(both, None),
    )
    return jax.shard_map(
        functools.partial(body, (nx, ny, nz, granules)),
        mesh=mesh, in_specs=placed, out_specs=(P(both, None), P()), check_vma=False,
    )
```

time: 593 us -> 73.1 us (0.12)
  waiting for transfers between devices: 492 us -> 0 us
  Pallas kernels: 0 us -> 60 us
  starting transfers between devices: 38.9 us -> 0 us
  matrix products: 26 us -> 0 us
  between operations: 14.3 us -> 0.65 us
  other arithmetic: 12 us -> 0 us
    psum x1 -> x0, waiting for transfers between devices: 461 us -> none  [body(): summed = lax.psum(local_term, ('grp', 'dom'))]
    pallas_call x0 -> x1, Pallas kernels: none -> 60 us  [body(): pl.pallas_call(functools.partial(kernel, sizes, scale), out_shape=(jax.Sh...]
    all_to_all x4 -> x0, starting transfers between devices: 38.8 us -> none  [the longest x1 15.7 us: body(): lax.all_to_all(outer_sums.astype(jnp.bfloat16), 'grp', split_axis=0, conc...]
    all_to_all x4 -> x0, waiting for transfers between devices: 31 us -> none  [the longest x1 16.8 us: body(): lax.all_to_all(inner_sums, 'dom', split_axis=0, concat_axis=0, tiled=True)]
    dot_general x7 -> x0, matrix products: 26 us -> none  [the longest x2 15.3 us: tile_step(): jnp.einsum('kc,kjf->cjf', selector, product, precision=lax.Precision.HIGH...]
    unnamed x20 -> x24, local copies, waits for them, and re-layouts: 0.23 us -> 12.1 us
  transfers between devices with their start and end apart: 5 -> 0, of which waited for: 4 -> 0; matrix products, arithmetic and copies ran while one was open for 1% -> 0% of each run, Pallas kernels for 0% -> 0%
where the time goes in v1:
time: 73.1 us; the launch traced here: 72.7 us
  Pallas kernels  60 us (82%)
  local copies, waits for them, and re-layouts  12.1 us (17%)
    pallas_call x1, Pallas kernels, body(): pl.pallas_call(functools.partial(kernel, sizes, scale), out_shape=(jax.Sh...  60 us
    unnamed x24, local copies, waits for them, and re-layouts  12.1 us

profile of v1, /device:TPU:1, one launch (start us, length us, event | category | flops | bytes accessed | tf_op | source)
XLA Modules:
  0.0 72.7 jit_solution(2576650921973798442)
XLA Ops:
  0.6 0.8 %copy.15.xrow = s32[1,12,4]{2,1,0:T(8,128)S(1)} copy(s32[1,12,4]{1,2,0:T(4,128)} %param.22) | data formatting | bytes 384 | tf_op args[10]
  1.4 0.8 %copy.14.mrow = s32[1,64,8]{2,1,0:T(8,128)S(1)} copy(s32[1,64,8]{1,2,0:T(8,128)} %param.20) | data formatting | bytes 4096 | tf_op args[8]
  2.2 0.0 copy-start
  2.2 1.6 %copy-done = bf16[64,128,128]{2,1,0:T(8,128)(2,1)S(1)} copy-done((bf16[64,128,128]{2,1,0:T(8,128)(2,1)S(1)}, bf16[64,128,128]{2,1,0:T(8,128)(2,1)}, u32[]{:S(2)}) %copy-start) | copy-done | bytes 2097176
  3.8 0.0 copy-start.1
  3.8 1.1 %copy-done.1 = bf16[1152,256]{1,0:T(8,128)(2,1)S(1)} copy-done((bf16[1152,256]{1,0:T(8,128)(2,1)S(1)}, bf16[1152,256]{1,0:T(8,128)(2,1)}, u32[]{:S(2)}) %copy-start.1) | copy-done | bytes 589848
  4.8 0.0 copy-start.2
  4.8 0.9 %copy-done.2 = bf16[512,256]{1,0:T(8,128)(2,1)S(1)} copy-done((bf16[512,256]{1,0:T(8,128)(2,1)S(1)}, bf16[512,256]{1,0:T(8,128)(2,1)}, u32[]{:S(2)}) %copy-start.2) | copy-done | bytes 262168
  5.8 0.0 copy-start.3
  5.8 0.9 %copy-done.3 = bf16[512,256]{1,0:T(8,128)(2,1)S(1)} copy-done((bf16[512,256]{1,0:T(8,128)(2,1)S(1)}, bf16[512,256]{1,0:T(8,128)(2,1)}, u32[]{:S(2)}) %copy-start.3) | copy-done | bytes 262168
  6.7 0.0 copy-start.4
  6.7 0.9 %copy-done.4 = bf16[256,256]{1,0:T(8,128)(2,1)S(1)} copy-done((bf16[256,256]{1,0:T(8,128)(2,1)S(1)}, bf16[256,256]{1,0:T(8,128)(2,1)}, u32[]{:S(2)}) %copy-start.4) | copy-done | bytes 131096
  7.6 0.0 copy-start.5
  7.6 0.9 %copy-done.5 = bf16[256,256]{1,0:T(8,128)(2,1)S(1)} copy-done((bf16[256,256]{1,0:T(8,128)(2,1)S(1)}, bf16[256,256]{1,0:T(8,128)(2,1)}, u32[]{:S(2)}) %copy-start.5) | copy-done | bytes 131096
  8.5 0.0 copy-start.6
  8.5 0.7 copy-done.6
  9.2 0.0 copy-start.7
  9.2 0.7 copy-done.7
  9.8 0.0 copy-start.8
  9.9 0.7 copy-done.8
  10.5 0.0 copy-start.9
  10.5 0.7 copy-done.9
  11.2 60.0 %shard_map.131 = (bf16[1152,256]{1,0:T(8,128)(2,1)S(1)}, f32[2,256,256]{2,1,0:T(8,128)S(1)}) custom-call(bf16[1152,256]{1,0:T(8,128)(2,1)S(1)} %copy-done.1, bf16[512,256]{1,0:T(8,128)(2,1)S(1)} %copy-done.2, bf16[512,256]{1,0:T(8,128)(2,1)S(1)} %copy-done.3, bf16[256,256]{1,0:T(8,128)(2,1)S(1)} %copy-done.4, bf16[256,256]{1,0:T(8,128)(2,1)S(1)} %copy-done.5, ...), custom_call_target="tpu_custom_call" | custom-call | tf_op jit(solution)/shard_map/pallas_call | solution.py:354
  71.1 0.8 %copy.18 = bf16[1152,256]{1,0:T(8,128)(2,1)} copy(bf16[1152,256]{1,0:T(8,128)(2,1)S(1)} %get-tuple-element.4) | data formatting | bytes 1179648
  71.9 0.8 %copy.19 = f32[2,256,256]{2,1,0:T(8,128)} copy(f32[2,256,256]{2,1,0:T(8,128)S(1)} %get-tuple-element.5) | data formatting | bytes 1048576
Async XLA Ops:
  2.2 1.6 %copy-start = (bf16[64,128,128]{2,1,0:T(8,128)(2,1)S(1)}, bf16[64,128,128]{2,1,0:T(8,128)(2,1)}, u32[]{:S(2)}) copy-start(bf16[64,128,128]{2,1,0:T(8,128)(2,1)} %tiles_hbm.1) | copy-start | bytes 6291460
  3.8 1.1 %copy-start.1 = (bf16[1152,256]{1,0:T(8,128)(2,1)S(1)}, bf16[1152,256]{1,0:T(8,128)(2,1)}, u32[]{:S(2)}) copy-start(bf16[1152,256]{1,0:T(8,128)(2,1)} %cot_hbm.1) | copy-start | bytes 1769476
  4.8 0.9 %copy-start.2 = (bf16[512,256]{1,0:T(8,128)(2,1)S(1)}, bf16[512,256]{1,0:T(8,128)(2,1)}, u32[]{:S(2)}) copy-start(bf16[512,256]{1,0:T(8,128)(2,1)} %feat_hbm.1) | copy-start | bytes 786436
  5.8 0.9 %copy-start.3 = (bf16[512,256]{1,0:T(8,128)(2,1)S(1)}, bf16[512,256]{1,0:T(8,128)(2,1)}, u32[]{:S(2)}) copy-start(bf16[512,256]{1,0:T(8,128)(2,1)} %agg_hbm.1) | copy-start | bytes 786436
  6.7 0.9 %copy-start.4 = (bf16[256,256]{1,0:T(8,128)(2,1)S(1)}, bf16[256,256]{1,0:T(8,128)(2,1)}, u32[]{:S(2)}) copy-start(bf16[256,256]{1,0:T(8,128)(2,1)} %wself_hbm.1) | copy-start | bytes 393220
  7.6 0.9 %copy-start.5 = (bf16[256,256]{1,0:T(8,128)(2,1)S(1)}, bf16[256,256]{1,0:T(8,128)(2,1)}, u32[]{:S(2)}) copy-start(bf16[256,256]{1,0:T(8,128)(2,1)} %wneigh_hbm.1) | copy-start | bytes 393220
  8.5 0.7 copy-start.6
  9.2 0.7 copy-start.7
  9.8 0.7 copy-start.8
  10.5 0.7 copy-start.9

commit v2 on v1

v2 whole, which is shorter than its diff:
```python
import functools
import math

import jax
import jax.numpy as jnp
from jax import lax
from jax.experimental import pallas as pl
from jax.experimental.pallas import tpu as pltpu
from jax.sharding import PartitionSpec as P

F32 = jnp.float32
BF16 = jnp.bfloat16
MESH = pl.DeviceIdType.MESH
UNROLL = 8
RS_TYPE = BF16
AG_TYPE = BF16
VMEM_LIMIT = 60 * 1024 * 1024


def dot_tt(left, right):
    return lax.dot_general(left, right, (((1,), (1,)), ((), ())), preferred_element_type=F32)


def dot_nn(left, right):
    return lax.dot_general(left, right, (((1,), (0,)), ((), ())), preferred_element_type=F32)


def dot_tn(left, right):
    return lax.dot_general(left, right, (((0,), (0,)), ((), ())), preferred_element_type=F32)


def iota(shape, axis):
    return lax.broadcasted_iota(jnp.int32, shape, axis)


def one_hot(mask):
    return jnp.where(mask, 1.0, 0.0).astype(F32)


def list_lanes(rows_ref, count_ref, lanes):
    capacity, peers = rows_ref.shape[1], rows_ref.shape[2]
    mine = iota((peers, lanes), 1) // 8 == iota((peers, lanes), 0)
    spread = lax.dot_general(
        rows_ref[0].astype(F32), one_hot(mine), (((1,), (0,)), ((), ())),
        precision=lax.Precision.HIGHEST, preferred_element_type=F32,
    )
    entry = iota((capacity, lanes), 1) % 8 == iota((capacity, lanes), 0)
    rows = jnp.sum(jnp.where(entry, spread, 0.0), axis=0, keepdims=True)
    counts = lax.dot_general(
        count_ref[...].astype(F32), one_hot(mine), (((1,), (0,)), ((), ())),
        precision=lax.Precision.HIGHEST, preferred_element_type=F32,
    )
    live = (iota((1, lanes), 1) % 8).astype(F32) < counts
    return jnp.where(live, rows, -1.0)


def to_chunks(rows, size=8):
    count, half = rows.shape[0] // size, rows.shape[1] // 2
    left = rows[:, :half].reshape(count, size, half)
    right = rows[:, half:].reshape(count, size, half)
    return jnp.concatenate([left, right], axis=1).astype(BF16)


def from_chunks(chunks):
    count, size, half = chunks.shape[0], chunks.shape[1] // 2, chunks.shape[2]
    wide = chunks.astype(F32)
    left = wide[:, :size].reshape(count * size, half)
    right = wide[:, size:].reshape(count * size, half)
    return jnp.concatenate([left, right], axis=1)


def kernel(
    sizes, scale,
    cot_hbm, feat_hbm, agg_hbm, wself_hbm, wneigh_hbm, tiles_hbm,
    trow_hbm, tcol_hbm, mrow_hbm, mcnt_hbm, xrow_hbm, xcnt_hbm,
    slots_out, weights_out,
    cot, feat, agg, wself, wneigh, tiles, trow, tcol, mrow, mcnt, xrow, xcnt, grads, run, part, own, slots,
    pick, pick_t, send_a, recv_a, send_b, recv_b,
    sendx_a, recvx_a, sendx_b, recvx_b,
    w_local, w_pair, w_rs, w_rsin, w_zin, w_ag, w_other, w_out,
    load_sem, store_sem, ex_sem, w_send, w_recv,
):
    nx, ny, nz = sizes
    nd = nx * ny * 2
    masters = feat.shape[0]
    chips = nx * ny
    grain = w_zin.shape[1]
    blocks = grads.shape[0]
    tile_total = tiles.shape[0]
    inner_end = masters + nd * 8
    z = lax.axis_index("grp")
    d = lax.axis_index("dom")
    core = d % 2
    y = (d // 2) % ny
    x = d // (2 * ny)
    chip = x * ny + y

    def away(place, length):
        return length // 2 + (place + 1) // 2 * (place % 2 * 2 - 1)

    def dom_of(xx, yy, cc):
        return (xx * ny + yy) * 2 + cc

    def hop(offset):
        return dom_of(
            (x + away(offset // 2 % nx, nx)) % nx,
            (y + away(offset // (2 * nx), ny)) % ny,
            (core + 1 - offset % 2) % 2,
        )

    def chip_hop(offset):
        return (x + away(offset % nx, nx)) % nx * ny + (y + away(offset // nx, ny)) % ny

    loads = []
    for place, (src, dst) in enumerate(
        [(cot_hbm, cot), (feat_hbm, feat), (agg_hbm, agg), (wneigh_hbm, wneigh),
         (trow_hbm, trow), (tcol_hbm, tcol), (tiles_hbm, tiles), (wself_hbm, wself),
         (mrow_hbm, mrow), (mcnt_hbm, mcnt), (xrow_hbm, xrow), (xcnt_hbm, xcnt)]
    ):
        load = pltpu.make_async_copy(src, dst, load_sem.at[place])
        load.start()
        loads.append(load)

    barrier = pltpu.get_barrier_semaphore()

    @pl.loop(0, nd - 1)
    def _(offset):
        pl.semaphore_signal(barrier, inc=1, device_id=(z, hop(offset)), device_id_type=MESH)

    @pl.loop(1, nz)
    def _(offset):
        pl.semaphore_signal(
            barrier, inc=1, device_id=((z + offset) % nz, d), device_id_type=MESH
        )

    def push(src, dst, stage, target):
        copy = pltpu.make_async_remote_copy(
            src_ref=src, dst_ref=dst, send_sem=w_send.at[stage], recv_sem=w_recv.at[stage],
            device_id=target, device_id_type=MESH,
        )
        copy.start()

    stores = []

    def store(src, dst, place):
        copy = pltpu.make_async_copy(src, dst, store_sem.at[place])
        copy.start()
        stores.append(copy)

    def settle(ref, sem):
        pltpu.make_async_copy(ref, ref, sem).wait()

    loads[0].wait()
    loads[1].wait()
    w_local[0] = dot_tn(feat[...], cot[:masters])
    loads[2].wait()
    w_local[1] = dot_tn(agg[...], cot[:masters])

    loads[3].wait()
    for block in range(blocks):
        rows = slice(block * 128, block * 128 + 128)
        grads[block] = dot_tt(cot[rows], wneigh[...]).astype(BF16)

    pl.semaphore_wait(barrier, nd - 1 + nz - 1)
    partner = (z, d + 1 - 2 * core)
    push(w_local.at[1 - core], w_pair, 0, partner)

    run[0] = jnp.zeros(run.shape[1:], F32)
    for load in loads[4:7]:
        load.wait()

    def tile_group(group, last):
        for step in range(UNROLL):
            k = group * UNROLL + step
            column = tcol[k]
            before = last[0]
            for block in range(1, blocks):
                before = jnp.where(column == block, last[block], before)
            product = dot_tn(tiles[k], grads[trow[k]])
            run[k + 1] = product + run[before]
            last = tuple(
                jnp.where(column == block, k + 1, last[block]) for block in range(blocks)
            )
        return last

    groups = tile_total // UNROLL
    last = tuple(jnp.int32(0) for _ in range(blocks))
    last = lax.fori_loop(0, groups // 2, tile_group, last)

    settle(w_pair, w_recv.at[0])
    if RS_TYPE == BF16:
        w_rs[...] = to_chunks(w_local[core] + w_pair[...], grain)
    else:
        w_rs[...] = (w_local[core] + w_pair[...]).reshape(w_rs.shape)

    @pl.loop(0, chips - 1)
    def _(offset):
        target = chip_hop(offset)
        push(w_rs.at[target], w_rsin.at[chip], 1, (z, target * 2 + core))

    w_rsin[chip] = w_rs[chip]
    last = lax.fori_loop(groups // 2, groups, tile_group, last)
    for block in range(blocks):
        part[block * 128:block * 128 + 128] = run[last[block]]

    send_a[...] = to_chunks(part[masters:inner_end])
    spread = (iota((128, 128), 0) // 8 == iota((128, 128), 1) // 4) & (
        iota((128, 128), 0) % 8 == iota((128, 128), 1) % 4
    ) & (iota((128, 128), 1) < nz * 4)
    sendx_a[...] = to_chunks(
        dot_nn(one_hot(spread).astype(BF16), part[inner_end:inner_end + 128].astype(BF16))
    )

    def exchange(send, recv, sendx, recvx, stage):
        @pl.loop(0, nd - 1)
        def _(offset):
            target = hop(offset)
            pltpu.make_async_remote_copy(
                src_ref=send.at[target], dst_ref=recv.at[d],
                send_sem=ex_sem.at[stage + 2], recv_sem=ex_sem.at[stage + 3],
                device_id=(z, target), device_id_type=MESH,
            ).start()

        @pl.loop(1, nz)
        def _(offset):
            target = (z + offset) % nz
            pltpu.make_async_remote_copy(
                src_ref=sendx.at[target], dst_ref=recvx.at[z],
                send_sem=ex_sem.at[stage], recv_sem=ex_sem.at[stage + 1],
                device_id=(target, d), device_id_type=MESH,
            ).start()

        recv[d] = send[d]
        recvx[z] = sendx[z]
        for slot in range(nz, recvx.shape[0]):
            recvx[slot] = jnp.zeros(recvx.shape[1:], BF16)

    def arrived(recv, recvx, stage):
        settle(recvx.at[pl.ds(0, nz - 1)], ex_sem.at[stage + 1])
        settle(recv.at[pl.ds(0, nd - 1)], ex_sem.at[stage + 3])

    def sent(send, sendx, stage):
        settle(sendx.at[pl.ds(0, nz - 1)], ex_sem.at[stage])
        settle(send.at[pl.ds(0, nd - 1)], ex_sem.at[stage + 2])

    exchange(send_a, recv_a, sendx_a, recvx_a, 0)

    for load in loads[7:]:
        load.wait()
    own[...] = dot_tt(cot[:masters], wself[...]) + part[:masters]
    inner_lanes = pick.shape[1] - 128
    lanes = jnp.concatenate(
        [list_lanes(mrow, mcnt, inner_lanes), list_lanes(xrow, xcnt, 128)], axis=1
    )
    master_of = iota(pick.shape, 0).astype(F32)
    pick[...] = one_hot(master_of == lanes).astype(BF16)

    slots_t = jnp.transpose(jnp.broadcast_to(lanes, (128, lanes.shape[1])))
    for block in range(masters // 128):
        columns = slice(block * 128, block * 128 + 128)
        master_at = (iota(slots_t.shape, 1) + block * 128).astype(F32)
        pick_t[:, columns] = one_hot(slots_t == master_at).astype(BF16)

    settle(w_rsin.at[pl.ds(0, chips - 1)], w_recv.at[1])
    terms = w_rsin[...]
    if RS_TYPE == BF16:
        terms = from_chunks(terms).reshape(chips, grain, w_zin.shape[2])
    w_zin[z] = jnp.sum(terms, axis=0)

    @pl.loop(0, nz - 1)
    def _(offset):
        push(w_zin.at[z], w_zin.at[z], 2, ((z + away(offset, nz)) % nz, d))

    arrived(recv_a, recvx_a, 0)
    back = jnp.concatenate([from_chunks(recv_a[...]), from_chunks(recvx_a[...])], axis=0).astype(BF16)
    master = (own[...] + dot_nn(pick[...], back)).astype(BF16)
    copies = dot_nn(pick_t[...], master)
    send_b[...] = to_chunks(copies[:inner_lanes])
    sendx_b[...] = to_chunks(copies[inner_lanes:])
    exchange(send_b, recv_b, sendx_b, recvx_b, 4)
    slots[:masters] = master
    store(slots.at[pl.ds(0, masters)], slots_out.at[pl.ds(0, masters)], 0)

    settle(w_zin.at[pl.ds(0, nz - 1)], w_recv.at[2])
    total = w_zin[0]
    for step in range(1, nz):
        total = total + w_zin[step]
    total = total * scale
    if AG_TYPE == BF16:
        total = to_chunks(total, grain)[0]
    w_ag[chip] = total

    @pl.loop(0, chips - 1)
    def _(offset):
        push(w_ag.at[chip], w_ag.at[chip], 3, (z, chip_hop(offset) * 2 + core))

    settle(w_ag.at[pl.ds(0, chips - 1)], w_recv.at[3])
    push(w_ag, w_other, 4, partner)

    def whole(part):
        return from_chunks(part[...]) if AG_TYPE == BF16 else part[...].reshape(w_out.shape[1:])

    w_out[0] = whole(w_ag)
    store(w_out.at[0], weights_out.at[core], 1)

    arrived(recv_b, recvx_b, 4)
    slots[masters:inner_end] = from_chunks(recv_b[...]).astype(BF16)
    gather = (iota((128, 128), 1) // 8 == iota((128, 128), 0) // 4) & (
        iota((128, 128), 1) % 8 == iota((128, 128), 0) % 4
    ) & (iota((128, 128), 0) < nz * 4)
    slots[inner_end:inner_end + 128] = dot_nn(
        one_hot(gather).astype(BF16), from_chunks(recvx_b[...]).astype(BF16)
    ).astype(BF16)
    tail = slots.shape[0] - inner_end - 128
    if tail:
        slots[inner_end + 128:] = jnp.zeros((tail, slots.shape[1]), BF16)
    rest = pl.ds(masters, slots.shape[0] - masters)
    store(slots.at[rest], slots_out.at[rest], 3)

    settle(w_other, w_recv.at[4])
    w_out[1] = whole(w_other)
    store(w_out.at[1], weights_out.at[1 - core], 2)

    for copy in stores:
        copy.wait()

    sent(send_a, sendx_a, 0)
    sent(send_b, sendx_b, 4)
    settle(w_pair, w_send.at[0])
    settle(w_rsin.at[pl.ds(0, chips - 1)], w_send.at[1])
    settle(w_zin.at[pl.ds(0, nz - 1)], w_send.at[2])
    settle(w_ag.at[pl.ds(0, chips - 1)], w_send.at[3])
    settle(w_other, w_send.at[4])


def hand_on(slots_in, weights_in, slots_out, weights_out, slots, weights, in_sem, out_sem):
    quarter = slots_in.shape[0] // 4
    pieces = [
        (weights_in.at[half], weights.at[half], weights_out.at[half]) for half in range(2)
    ] + [
        tuple(ref.at[pl.ds(place * quarter, quarter)] for ref in (slots_in, slots, slots_out))
        for place in range(4)
    ]
    taken = [
        pltpu.make_async_copy(src, mid, in_sem.at[place])
        for place, (src, mid, _) in enumerate(pieces)
    ]
    given = [
        pltpu.make_async_copy(mid, dst, out_sem.at[place])
        for place, (_, mid, dst) in enumerate(pieces)
    ]
    for copy in taken:
        copy.start()
    for arrived, copy in zip(taken, given):
        arrived.wait()
        copy.start()
    for copy in given:
        copy.wait()


def body(
    sizes,
    cotangent, features, aggregated, w_self, w_neigh, edge_tiles,
    tile_rows, tile_cols, mirror_rows, mirror_count, cross_rows, cross_count,
):
    nx, ny, nz = sizes
    nd = nx * ny * 2
    mirror_rows = jnp.swapaxes(mirror_rows, 1, 2)
    cross_rows = jnp.swapaxes(cross_rows, 1, 2)
    slot_count, width = cotangent.shape
    masters = features.shape[0]
    tile_total = edge_tiles.shape[0]
    blocks = slot_count // 128
    scale = 1.0 / math.sqrt(masters * nd * nz)
    grain = width // (nx * ny)
    wide = (nx * ny, grain, width)
    narrow = (nx * ny, 2 * grain, width // 2)
    rs_shape = narrow if RS_TYPE == BF16 else wide
    ag_shape = narrow if AG_TYPE == BF16 else wide
    hbm = pl.BlockSpec(memory_space=pltpu.HBM)
    lanes = (nd * 8 + 127) // 128 * 128 + 128
    chunk = (16, width // 2)
    dma = pltpu.SemaphoreType.DMA
    outs = (
        jax.ShapeDtypeStruct((slot_count, width), BF16),
        jax.ShapeDtypeStruct((2, width, width), F32),
    )
    found = pl.pallas_call(
        functools.partial(kernel, sizes, scale),
        out_shape=outs,
        in_specs=[hbm] * 12,
        out_specs=(hbm, hbm),
        scratch_shapes=[
            pltpu.VMEM(cotangent.shape, BF16),
            pltpu.VMEM(features.shape, BF16),
            pltpu.VMEM(aggregated.shape, BF16),
            pltpu.VMEM(w_self.shape, BF16),
            pltpu.VMEM(w_neigh.shape, BF16),
            pltpu.VMEM(edge_tiles.shape, BF16),
            pltpu.SMEM(tile_rows.shape, jnp.int32),
            pltpu.SMEM(tile_cols.shape, jnp.int32),
            pltpu.VMEM(mirror_rows.shape, jnp.int32),
            pltpu.VMEM(mirror_count.shape, jnp.int32),
            pltpu.VMEM(cross_rows.shape, jnp.int32),
            pltpu.VMEM(cross_count.shape, jnp.int32),
            pltpu.VMEM((blocks, 128, width), BF16),
            pltpu.VMEM((tile_total + 1, 128, width), F32),
            pltpu.VMEM((slot_count, width), F32),
            pltpu.VMEM((masters, width), F32),
            pltpu.VMEM((slot_count, width), BF16),
            pltpu.VMEM((masters, lanes), BF16),
            pltpu.VMEM((lanes, masters), BF16),
            pltpu.VMEM((nd,) + chunk, BF16),
            pltpu.VMEM((nd,) + chunk, BF16),
            pltpu.VMEM((nd,) + chunk, BF16),
            pltpu.VMEM((nd,) + chunk, BF16),
            pltpu.VMEM((16,) + chunk, BF16),
            pltpu.VMEM((16,) + chunk, BF16),
            pltpu.VMEM((16,) + chunk, BF16),
            pltpu.VMEM((16,) + chunk, BF16),
            pltpu.VMEM((2, width, width), F32),
            pltpu.VMEM((width, width), F32),
            pltpu.VMEM(rs_shape, RS_TYPE),
            pltpu.VMEM(rs_shape, RS_TYPE),
            pltpu.VMEM((nz, grain, width), F32),
            pltpu.VMEM(ag_shape, AG_TYPE),
            pltpu.VMEM(ag_shape, AG_TYPE),
            pltpu.VMEM((2, width, width), F32),
            dma((12,)),
            dma((4,)),
            dma((8,)),
            dma((5,)),
            dma((5,)),
        ],
        compiler_params=pltpu.CompilerParams(
            collective_id=0, has_side_effects=True, vmem_limit_bytes=VMEM_LIMIT
        ),
    )(
        cotangent, features, aggregated, w_self, w_neigh, edge_tiles,
        tile_rows, tile_cols, mirror_rows, mirror_count, cross_rows, cross_count,
    )
    return pl.pallas_call(
        hand_on,
        out_shape=outs,
        in_specs=[hbm, hbm],
        out_specs=(hbm, hbm),
        scratch_shapes=[
            pltpu.VMEM(outs[0].shape, BF16), pltpu.VMEM(outs[1].shape, F32), dma((6,)), dma((6,)),
        ],
        compiler_params=pltpu.CompilerParams(vmem_limit_bytes=VMEM_LIMIT),
    )(*found)


def solution(mesh, grid=(4, 8)):
    nx, ny = grid
    nz = mesh.shape["grp"]
    both = ("grp", "dom")
    placed = (
        P(both, None), P(both, None), P(both, None), P(), P(), P(both, None, None),
        P(both), P(both), P(both, None, None), P(both, None), P(both, None, None),
        P(both, None),
    )
    return jax.shard_map(
        functools.partial(body, (nx, ny, nz)),
        mesh=mesh, in_specs=placed, out_specs=(P(both, None), P()), check_vma=False,
    )
```

time: 73.1 us -> 55.1 us (0.75)
  local copies, waits for them, and re-layouts: 12.1 us -> 0 us
  Pallas kernels: 60 us -> 54.3 us
    unnamed x24 -> x0, local copies, waits for them, and re-layouts: 12.1 us -> none
    pallas_call x1 -> x2, Pallas kernels: 60 us -> 54.3 us  [the longest x1 52.3 us: body(): pl.pallas_call(functools.partial(kernel, sizes, scale), out_shape=outs, i...]
where the time goes in v2:
time: 55.1 us; the launch traced here: 54.9 us
  Pallas kernels  54.3 us (99%)
  between operations  0.64 us (1%)
    pallas_call x1, Pallas kernels, body(): pl.pallas_call(functools.partial(kernel, sizes, scale), out_shape=outs, i...  52.3 us
    pallas_call x1, Pallas kernels, body(): pl.pallas_call(hand_on, out_shape=outs, in_specs=[hbm, hbm], out_specs=(h...  2.03 us

profile of v2, /device:TPU:1, one launch (start us, length us, event | category | flops | bytes accessed | tf_op | source)
XLA Modules:
  0.0 54.9 jit_solution(6823562181428320751)
XLA Ops:
  0.6 52.3 %shard_map.131 = (bf16[1152,256]{1,0:T(8,128)(2,1)}, f32[2,256,256]{2,1,0:T(8,128)}) custom-call(bf16[1152,256]{1,0:T(8,128)(2,1)} %cot_hbm.1, bf16[512,256]{1,0:T(8,128)(2,1)} %feat_hbm.1, bf16[512,256]{1,0:T(8,128)(2,1)} %agg_hbm.1, bf16[256,256]{1,0:T(8,128)(2,1)} %wself_hbm.1, bf16[256,256]{1,0:T(8,128)(2,1)} %wneigh_hbm.1, ...), custom_call_target="tpu_custom_call" | custom-call | tf_op jit(solution)/shard_map/pallas_call | solution.py:388
  52.9 2.0 %shard_map.132 = (bf16[1152,256]{1,0:T(8,128)(2,1)}, f32[2,256,256]{2,1,0:T(8,128)}) custom-call(bf16[1152,256]{1,0:T(8,128)(2,1)} %get-tuple-element.4.slots_in, f32[2,256,256]{2,1,0:T(8,128)} %get-tuple-element.5.weights_in), custom_call_target="tpu_custom_call" | custom-call | tf_op jit(solution)/shard_map/pallas_call | solution.py:442

commit v3 on v2

--- a/solution.py
+++ b/solution.py
@@ -12,8 +12,7 @@
 BF16 = jnp.bfloat16
 MESH = pl.DeviceIdType.MESH
 UNROLL = 8
-RS_TYPE = BF16
-AG_TYPE = BF16
+Z_TYPE = F32
 VMEM_LIMIT = 60 * 1024 * 1024
 
 
@@ -73,18 +72,17 @@
     sizes, scale,
     cot_hbm, feat_hbm, agg_hbm, wself_hbm, wneigh_hbm, tiles_hbm,
     trow_hbm, tcol_hbm, mrow_hbm, mcnt_hbm, xrow_hbm, xcnt_hbm,
-    slots_out, weights_out,
-    cot, feat, agg, wself, wneigh, tiles, trow, tcol, mrow, mcnt, xrow, xcnt, grads, run, part, own, slots,
-    pick, pick_t, send_a, recv_a, send_b, recv_b,
-    sendx_a, recvx_a, sendx_b, recvx_b,
-    w_local, w_pair, w_rs, w_rsin, w_zin, w_ag, w_other, w_out,
+    master_out, recv_b, recvx_b, w_out,
+    cot, feat, agg, wself, wneigh, tiles, trow, tcol, mrow, mcnt, xrow, xcnt, grads, run, part, own, master,
+    pick, pick_t, send_a, recv_a, send_b, sendx_a, recvx_a, sendx_b,
+    w_local, w_pair, w_rs, w_rsin, w_zin, w_ag,
     load_sem, store_sem, ex_sem, w_send, w_recv,
 ):
     nx, ny, nz = sizes
     nd = nx * ny * 2
     masters = feat.shape[0]
     chips = nx * ny
-    grain = w_zin.shape[1]
+    grain = w_zin.shape[1] // 2
     blocks = grads.shape[0]
     tile_total = tiles.shape[0]
     inner_end = masters + nd * 8
@@ -113,8 +111,8 @@
 
     loads = []
     for place, (src, dst) in enumerate(
-        [(cot_hbm, cot), (feat_hbm, feat), (agg_hbm, agg), (wneigh_hbm, wneigh),
-         (trow_hbm, trow), (tcol_hbm, tcol), (tiles_hbm, tiles), (wself_hbm, wself),
+        [(cot_hbm, cot), (wneigh_hbm, wneigh), (trow_hbm, trow), (tcol_hbm, tcol),
+         (tiles_hbm, tiles), (feat_hbm, feat), (agg_hbm, agg), (wself_hbm, wself),
          (mrow_hbm, mrow), (mcnt_hbm, mcnt), (xrow_hbm, xrow), (xcnt_hbm, xcnt)]
     ):
         load = pltpu.make_async_copy(src, dst, load_sem.at[place])
@@ -152,21 +150,12 @@
 
     loads[0].wait()
     loads[1].wait()
-    w_local[0] = dot_tn(feat[...], cot[:masters])
-    loads[2].wait()
-    w_local[1] = dot_tn(agg[...], cot[:masters])
-
-    loads[3].wait()
     for block in range(blocks):
         rows = slice(block * 128, block * 128 + 128)
         grads[block] = dot_tt(cot[rows], wneigh[...]).astype(BF16)
 
-    pl.semaphore_wait(barrier, nd - 1 + nz - 1)
-    partner = (z, d + 1 - 2 * core)
-    push(w_local.at[1 - core], w_pair, 0, partner)
-
     run[0] = jnp.zeros(run.shape[1:], F32)
-    for load in loads[4:7]:
+    for load in loads[2:5]:
         load.wait()
 
     def tile_group(group, last):
@@ -187,11 +176,22 @@
     last = tuple(jnp.int32(0) for _ in range(blocks))
     last = lax.fori_loop(0, groups // 2, tile_group, last)
 
+    loads[5].wait()
+    w_local[0] = dot_tn(feat[...], cot[:masters])
+    loads[6].wait()
+    w_local[1] = dot_tn(agg[...], cot[:masters])
+
+    pl.semaphore_wait(barrier, nd - 1 + nz - 1)
+    partner = (z, d + 1 - 2 * core)
+    push(w_local.at[1 - core], w_pair, 0, partner)
+
+    last = lax.fori_loop(groups // 2, groups, tile_group, last)
+    for block in range(blocks):
+        part[block * 128:block * 128 + 128] = run[last[block]]
+
+
     settle(w_pair, w_recv.at[0])
-    if RS_TYPE == BF16:
-        w_rs[...] = to_chunks(w_local[core] + w_pair[...], grain)
-    else:
-        w_rs[...] = (w_local[core] + w_pair[...]).reshape(w_rs.shape)
+    w_rs[...] = to_chunks(w_local[core] + w_pair[...], grain)
 
     @pl.loop(0, chips - 1)
     def _(offset):
@@ -199,10 +199,6 @@
         push(w_rs.at[target], w_rsin.at[chip], 1, (z, target * 2 + core))
 
     w_rsin[chip] = w_rs[chip]
-    last = lax.fori_loop(groups // 2, groups, tile_group, last)
-    for block in range(blocks):
-        part[block * 128:block * 128 + 128] = run[last[block]]
-
     send_a[...] = to_chunks(part[masters:inner_end])
     spread = (iota((128, 128), 0) // 8 == iota((128, 128), 1) // 4) & (
         iota((128, 128), 0) % 8 == iota((128, 128), 1) % 4
@@ -230,11 +226,6 @@
                 device_id=(target, d), device_id_type=MESH,
             ).start()
 
-        recv[d] = send[d]
-        recvx[z] = sendx[z]
-        for slot in range(nz, recvx.shape[0]):
-            recvx[slot] = jnp.zeros(recvx.shape[1:], BF16)
-
     def arrived(recv, recvx, stage):
         settle(recvx.at[pl.ds(0, nz - 1)], ex_sem.at[stage + 1])
         settle(recv.at[pl.ds(0, nd - 1)], ex_sem.at[stage + 3])
@@ -244,6 +235,10 @@
         settle(send.at[pl.ds(0, nd - 1)], ex_sem.at[stage + 2])
 
     exchange(send_a, recv_a, sendx_a, recvx_a, 0)
+    recv_a[d] = send_a[d]
+    recvx_a[z] = sendx_a[z]
+    for slot in range(nz, recvx_a.shape[0]):
+        recvx_a[slot] = jnp.zeros(recvx_a.shape[1:], BF16)
 
     for load in loads[7:]:
         load.wait()
@@ -262,10 +257,7 @@
         pick_t[:, columns] = one_hot(slots_t == master_at).astype(BF16)
 
     settle(w_rsin.at[pl.ds(0, chips - 1)], w_recv.at[1])
-    terms = w_rsin[...]
-    if RS_TYPE == BF16:
-        terms = from_chunks(terms).reshape(chips, grain, w_zin.shape[2])
-    w_zin[z] = jnp.sum(terms, axis=0)
+    w_zin[z] = jnp.sum(w_rsin[...].astype(F32), axis=0).astype(Z_TYPE)
 
     @pl.loop(0, nz - 1)
     def _(offset):
@@ -273,54 +265,31 @@
 
     arrived(recv_a, recvx_a, 0)
     back = jnp.concatenate([from_chunks(recv_a[...]), from_chunks(recvx_a[...])], axis=0).astype(BF16)
-    master = (own[...] + dot_nn(pick[...], back)).astype(BF16)
-    copies = dot_nn(pick_t[...], master)
+    master[...] = (own[...] + dot_nn(pick[...], back)).astype(BF16)
+    copies = dot_nn(pick_t[...], master[...])
     send_b[...] = to_chunks(copies[:inner_lanes])
     sendx_b[...] = to_chunks(copies[inner_lanes:])
-    exchange(send_b, recv_b, sendx_b, recvx_b, 4)
-    slots[:masters] = master
-    store(slots.at[pl.ds(0, masters)], slots_out.at[pl.ds(0, masters)], 0)
-
     settle(w_zin.at[pl.ds(0, nz - 1)], w_recv.at[2])
-    total = w_zin[0]
+    total = w_zin[0].astype(F32)
     for step in range(1, nz):
-        total = total + w_zin[step]
-    total = total * scale
-    if AG_TYPE == BF16:
-        total = to_chunks(total, grain)[0]
-    w_ag[chip] = total
+        total = total + w_zin[step].astype(F32)
+    w_ag[chip] = (total * scale).astype(BF16)
 
     @pl.loop(0, chips - 1)
     def _(offset):
         push(w_ag.at[chip], w_ag.at[chip], 3, (z, chip_hop(offset) * 2 + core))
 
+    exchange(send_b, recv_b, sendx_b, recvx_b, 4)
+    store(master, master_out, 0)
+    store(send_b.at[d], recv_b.at[d], 1)
+    store(sendx_b.at[z], recvx_b.at[z], 2)
+
     settle(w_ag.at[pl.ds(0, chips - 1)], w_recv.at[3])
-    push(w_ag, w_other, 4, partner)
-
-    def whole(part):
-        return from_chunks(part[...]) if AG_TYPE == BF16 else part[...].reshape(w_out.shape[1:])
-
-    w_out[0] = whole(w_ag)
-    store(w_out.at[0], weights_out.at[core], 1)
+    push(w_ag, w_out.at[core], 4, partner)
+    store(w_ag, w_out.at[core], 3)
 
     arrived(recv_b, recvx_b, 4)
-    slots[masters:inner_end] = from_chunks(recv_b[...]).astype(BF16)
-    gather = (iota((128, 128), 1) // 8 == iota((128, 128), 0) // 4) & (
-        iota((128, 128), 1) % 8 == iota((128, 128), 0) % 4
-    ) & (iota((128, 128), 0) < nz * 4)
-    slots[inner_end:inner_end + 128] = dot_nn(
-        one_hot(gather).astype(BF16), from_chunks(recvx_b[...]).astype(BF16)
-    ).astype(BF16)
-    tail = slots.shape[0] - inner_end - 128
-    if tail:
-        slots[inner_end + 128:] = jnp.zeros((tail, slots.shape[1]), BF16)
-    rest = pl.ds(masters, slots.shape[0] - masters)
-    store(slots.at[rest], slots_out.at[rest], 3)
-
-    settle(w_other, w_recv.at[4])
-    w_out[1] = whole(w_other)
-    store(w_out.at[1], weights_out.at[1 - core], 2)
-
+    settle(w_ag, w_recv.at[4])
     for copy in stores:
         copy.wait()
 
@@ -330,30 +299,46 @@
     settle(w_rsin.at[pl.ds(0, chips - 1)], w_send.at[1])
     settle(w_zin.at[pl.ds(0, nz - 1)], w_send.at[2])
     settle(w_ag.at[pl.ds(0, chips - 1)], w_send.at[3])
-    settle(w_other, w_send.at[4])
-
-
-def hand_on(slots_in, weights_in, slots_out, weights_out, slots, weights, in_sem, out_sem):
-    quarter = slots_in.shape[0] // 4
-    pieces = [
-        (weights_in.at[half], weights.at[half], weights_out.at[half]) for half in range(2)
-    ] + [
-        tuple(ref.at[pl.ds(place * quarter, quarter)] for ref in (slots_in, slots, slots_out))
-        for place in range(4)
-    ]
+    settle(w_ag, w_send.at[4])
+
+
+def finish(
+    nz, master_in, recv_in, recvx_in, w_in, slots_out, weights_out,
+    master, recv, recvx, parts, slots, weights, in_sem, out_sem,
+):
     taken = [
-        pltpu.make_async_copy(src, mid, in_sem.at[place])
-        for place, (src, mid, _) in enumerate(pieces)
-    ]
-    given = [
-        pltpu.make_async_copy(mid, dst, out_sem.at[place])
-        for place, (_, mid, dst) in enumerate(pieces)
+        pltpu.make_async_copy(src, dst, in_sem.at[place])
+        for place, (src, dst) in enumerate(
+            [(w_in, parts), (recv_in, recv), (master_in, master), (recvx_in, recvx)]
+        )
     ]
     for copy in taken:
         copy.start()
-    for arrived, copy in zip(taken, given):
-        arrived.wait()
+    masters, inner = master.shape[0], recv.shape[0] * 8
+    inner_end = masters + inner
+    given = []
+
+    def give(src, dst):
+        copy = pltpu.make_async_copy(src, dst, out_sem.at[len(given)])
         copy.start()
+        given.append(copy)
+
+    taken[0].wait()
+    for half in range(2):
+        weights[half] = from_chunks(parts[half])
+        give(weights.at[half], weights_out.at[half])
+    taken[1].wait()
+    slots[:inner] = from_chunks(recv[...]).astype(BF16)
+    give(slots.at[pl.ds(0, inner)], slots_out.at[pl.ds(masters, inner)])
+    taken[2].wait()
+    give(master, slots_out.at[pl.ds(0, masters)])
+    taken[3].wait()
+    lists = from_chunks(recvx[...]).astype(BF16)
+    tail = slots.shape[0] - inner
+    row, column = iota((tail, nz * 8), 0), iota((tail, nz * 8), 1)
+    gather = (column // 8 == row // 4) & (column % 8 == row % 4) & (row < nz * 4)
+    slots[inner:] = dot_nn(one_hot(gather).astype(BF16), lists).astype(BF16)
+    give(slots.at[pl.ds(inner, tail)], slots_out.at[pl.ds(inner_end, tail)])
     for copy in given:
         copy.wait()
 
@@ -373,10 +358,7 @@
     blocks = slot_count // 128
     scale = 1.0 / math.sqrt(masters * nd * nz)
     grain = width // (nx * ny)
-    wide = (nx * ny, grain, width)
     narrow = (nx * ny, 2 * grain, width // 2)
-    rs_shape = narrow if RS_TYPE == BF16 else wide
-    ag_shape = narrow if AG_TYPE == BF16 else wide
     hbm = pl.BlockSpec(memory_space=pltpu.HBM)
     lanes = (nd * 8 + 127) // 128 * 128 + 128
     chunk = (16, width // 2)
@@ -385,11 +367,17 @@
         jax.ShapeDtypeStruct((slot_count, width), BF16),
         jax.ShapeDtypeStruct((2, width, width), F32),
     )
+    landed = (
+        jax.ShapeDtypeStruct((masters, width), BF16),
+        jax.ShapeDtypeStruct((nd,) + chunk, BF16),
+        jax.ShapeDtypeStruct((nz,) + chunk, BF16),
+        jax.ShapeDtypeStruct((2,) + narrow, BF16),
+    )
     found = pl.pallas_call(
         functools.partial(kernel, sizes, scale),
-        out_shape=outs,
+        out_shape=landed,
         in_specs=[hbm] * 12,
-        out_specs=(hbm, hbm),
+        out_specs=(hbm,) * 4,
         scratch_shapes=[
             pltpu.VMEM(cotangent.shape, BF16),
             pltpu.VMEM(features.shape, BF16),
@@ -407,25 +395,21 @@
             pltpu.VMEM((tile_total + 1, 128, width), F32),
             pltpu.VMEM((slot_count, width), F32),
             pltpu.VMEM((masters, width), F32),
-            pltpu.VMEM((slot_count, width), BF16),
+            pltpu.VMEM((masters, width), BF16),
             pltpu.VMEM((masters, lanes), BF16),
             pltpu.VMEM((lanes, masters), BF16),
-            pltpu.VMEM((nd,) + chunk, BF16),
             pltpu.VMEM((nd,) + chunk, BF16),
             pltpu.VMEM((nd,) + chunk, BF16),
             pltpu.VMEM((nd,) + chunk, BF16),
             pltpu.VMEM((16,) + chunk, BF16),
             pltpu.VMEM((16,) + chunk, BF16),
             pltpu.VMEM((16,) + chunk, BF16),
-            pltpu.VMEM((16,) + chunk, BF16),
             pltpu.VMEM((2, width, width), F32),
             pltpu.VMEM((width, width), F32),
-            pltpu.VMEM(rs_shape, RS_TYPE),
-            pltpu.VMEM(rs_shape, RS_TYPE),
-            pltpu.VMEM((nz, grain, width), F32),
-            pltpu.VMEM(ag_shape, AG_TYPE),
-            pltpu.VMEM(ag_shape, AG_TYPE),
-            pltpu.VMEM((2, width, width), F32),
+            pltpu.VMEM(narrow, BF16),
+            pltpu.VMEM(narrow, BF16),
+            pltpu.VMEM((nz,) + narrow[1:], Z_TYPE),
+            pltpu.VMEM(narrow, BF16),
             dma((12,)),
             dma((4,)),
             dma((8,)),
@@ -440,12 +424,16 @@
         tile_rows, tile_cols, mirror_rows, mirror_count, cross_rows, cross_count,
     )
     return pl.pallas_call(
-        hand_on,
+        functools.partial(finish, nz),
         out_shape=outs,
-        in_specs=[hbm, hbm],
+        in_specs=[hbm] * 4,
         out_specs=(hbm, hbm),
-        scratch_shapes=[
-            pltpu.VMEM(outs[0].shape, BF16), pltpu.VMEM(outs[1].shape, F32), dma((6,)), dma((6,)),
+        scratch_shapes=[pltpu.VMEM(array.shape, array.dtype) for array in landed]
+        + [
+            pltpu.VMEM((slot_count - masters, width), BF16),
+            pltpu.VMEM(outs[1].shape, F32),
+            dma((4,)),
+            dma((5,)),
         ],
         compiler_params=pltpu.CompilerParams(vmem_limit_bytes=VMEM_LIMIT),
     )(*found)

time: 55.1 us -> 51.9 us (0.942)
  Pallas kernels: 54.3 us -> 51.1 us
    pallas_call x2, Pallas kernels: 54.3 us -> 51.1 us  [the longest x1 49.1 us: body(): pl.pallas_call(functools.partial(kernel, sizes, scale), out_shape=landed,...]
where the time goes in v3:
time: 51.9 us; the launch traced here: 51.7 us
  Pallas kernels  51.1 us (98%)
  between operations  0.64 us (1%)
    pallas_call x1, Pallas kernels, body(): pl.pallas_call(functools.partial(kernel, sizes, scale), out_shape=landed,...  49.1 us
    pallas_call x1, Pallas kernels, body(): pl.pallas_call(functools.partial(finish, nz), out_shape=outs, in_specs=[h...  2.02 us

profile of v3, /device:TPU:1, one launch (start us, length us, event | category | flops | bytes accessed | tf_op | source)
XLA Modules:
  0.0 51.7 jit_solution(16648789577332588590)
XLA Ops:
  0.6 49.1 %shard_map.131 = (bf16[512,256]{1,0:T(8,128)(2,1)}, bf16[64,16,128]{2,1,0:T(8,128)(2,1)}, bf16[12,16,128]{2,1,0:T(8,128)(2,1)}, bf16[2,32,16,128]{3,2,1,0:T(8,128)(2,1)}) custom-call(bf16[1152,256]{1,0:T(8,128)(2,1)} %cot_hbm.1, bf16[512,256]{1,0:T(8,128)(2,1)} %feat_hbm.1, bf16[512,256]{1,0:T(8,128)(2,1)} %agg_hbm.1, bf16[256,256]{1,0:T(8,128)(2,1)} %wself_hbm.1, ...), custom_call_target="tpu_custom_call" | custom-call | tf_op jit(solution)/shard_map/pallas_call | solution.py:376
  49.7 2.0 %shard_map.132 = (bf16[1152,256]{1,0:T(8,128)(2,1)}, f32[2,256,256]{2,1,0:T(8,128)}) custom-call(bf16[512,256]{1,0:T(8,128)(2,1)} %get-tuple-element.6.master_in, bf16[64,16,128]{2,1,0:T(8,128)(2,1)} %get-tuple-element.7.recv_in, bf16[12,16,128]{2,1,0:T(8,128)(2,1)} %get-tuple-element.8.recvx_in, bf16[2,32,16,128]{3,2,1,0:T(8,128)(2,1)} %get-tuple-element.9.w_in), custom_call_target="tpu_custom_call" | custom-call | tf_op jit(solution)/shard_map/pallas_call | solution.py:426

commit v4 on v3

--- a/solution.py
+++ b/solution.py
@@ -88,26 +88,42 @@
     inner_end = masters + nd * 8
     z = lax.axis_index("grp")
     d = lax.axis_index("dom")
-    core = d % 2
-    y = (d // 2) % ny
-    x = d // (2 * ny)
+    core = lax.rem(d, 2)
+    y = lax.rem(lax.div(d, 2), ny)
+    x = lax.div(d, 2 * ny)
     chip = x * ny + y
 
     def away(place, length):
         return length // 2 + (place + 1) // 2 * (place % 2 * 2 - 1)
 
-    def dom_of(xx, yy, cc):
-        return (xx * ny + yy) * 2 + cc
-
-    def hop(offset):
-        return dom_of(
-            (x + away(offset // 2 % nx, nx)) % nx,
-            (y + away(offset // (2 * nx), ny)) % ny,
-            (core + 1 - offset % 2) % 2,
-        )
-
-    def chip_hop(offset):
-        return (x + away(offset % nx, nx)) % nx * ny + (y + away(offset // nx, ny)) % ny
+    x_ahead = [lax.rem(x + away(step, nx), nx) * ny for step in range(nx)]
+
+    def each_chip(act, with_cores):
+        def column(y_there, last):
+            for step in range(nx):
+                there = (x_ahead[step] + y_there) * 2
+                own = last and step == nx - 1
+                if with_cores:
+                    act(there + 1 - core)
+                if not own:
+                    act(there + core)
+
+        @pl.loop(0, ny - 1)
+        def _(step):
+            column(lax.rem(y + away(step, ny), ny), False)
+
+        column(y, True)
+
+    def each_z(act):
+        for step in range(nz - 1):
+            act(lax.rem(z + away(step, nz), nz))
+
+    barrier = pltpu.get_barrier_semaphore()
+
+    def greet(target):
+        pl.semaphore_signal(barrier, inc=1, device_id=target, device_id_type=MESH)
+
+    each_z(lambda there: greet((there, d)))
 
     loads = []
     for place, (src, dst) in enumerate(
@@ -119,17 +135,7 @@
         load.start()
         loads.append(load)
 
-    barrier = pltpu.get_barrier_semaphore()
-
-    @pl.loop(0, nd - 1)
-    def _(offset):
-        pl.semaphore_signal(barrier, inc=1, device_id=(z, hop(offset)), device_id_type=MESH)
-
-    @pl.loop(1, nz)
-    def _(offset):
-        pl.semaphore_signal(
-            barrier, inc=1, device_id=((z + offset) % nz, d), device_id_type=MESH
-        )
+    each_chip(lambda there: greet((z, there)), True)
 
     def push(src, dst, stage, target):
         copy = pltpu.make_async_remote_copy(
@@ -190,15 +196,6 @@
         part[block * 128:block * 128 + 128] = run[last[block]]
 
 
-    settle(w_pair, w_recv.at[0])
-    w_rs[...] = to_chunks(w_local[core] + w_pair[...], grain)
-
-    @pl.loop(0, chips - 1)
-    def _(offset):
-        target = chip_hop(offset)
-        push(w_rs.at[target], w_rsin.at[chip], 1, (z, target * 2 + core))
-
-    w_rsin[chip] = w_rs[chip]
     send_a[...] = to_chunks(part[masters:inner_end])
     spread = (iota((128, 128), 0) // 8 == iota((128, 128), 1) // 4) & (
         iota((128, 128), 0) % 8 == iota((128, 128), 1) % 4
@@ -207,24 +204,31 @@
         dot_nn(one_hot(spread).astype(BF16), part[inner_end:inner_end + 128].astype(BF16))
     )
 
+    settle(w_pair, w_recv.at[0])
+    w_rs[...] = to_chunks(w_local[core] + w_pair[...], grain)
+
+    each_chip(
+        lambda there: push(w_rs.at[lax.div(there, 2)], w_rsin.at[chip], 1, (z, there)), False
+    )
+
+    w_rsin[chip] = w_rs[chip]
     def exchange(send, recv, sendx, recvx, stage):
-        @pl.loop(0, nd - 1)
-        def _(offset):
-            target = hop(offset)
+        def to_peer(target):
             pltpu.make_async_remote_copy(
                 src_ref=send.at[target], dst_ref=recv.at[d],
                 send_sem=ex_sem.at[stage + 2], recv_sem=ex_sem.at[stage + 3],
                 device_id=(z, target), device_id_type=MESH,
             ).start()
 
-        @pl.loop(1, nz)
-        def _(offset):
-            target = (z + offset) % nz
+        def to_group(target):
             pltpu.make_async_remote_copy(
                 src_ref=sendx.at[target], dst_ref=recvx.at[z],
                 send_sem=ex_sem.at[stage], recv_sem=ex_sem.at[stage + 1],
                 device_id=(target, d), device_id_type=MESH,
             ).start()
+
+        each_chip(to_peer, True)
+        each_z(to_group)
 
     def arrived(recv, recvx, stage):
         settle(recvx.at[pl.ds(0, nz - 1)], ex_sem.at[stage + 1])
@@ -259,9 +263,7 @@
     settle(w_rsin.at[pl.ds(0, chips - 1)], w_recv.at[1])
     w_zin[z] = jnp.sum(w_rsin[...].astype(F32), axis=0).astype(Z_TYPE)
 
-    @pl.loop(0, nz - 1)
-    def _(offset):
-        push(w_zin.at[z], w_zin.at[z], 2, ((z + away(offset, nz)) % nz, d))
+    each_z(lambda there: push(w_zin.at[z], w_zin.at[z], 2, (there, d)))
 
     arrived(recv_a, recvx_a, 0)
     back = jnp.concatenate([from_chunks(recv_a[...]), from_chunks(recvx_a[...])], axis=0).astype(BF16)
@@ -275,9 +277,7 @@
         total = total + w_zin[step].astype(F32)
     w_ag[chip] = (total * scale).astype(BF16)
 
-    @pl.loop(0, chips - 1)
-    def _(offset):
-        push(w_ag.at[chip], w_ag.at[chip], 3, (z, chip_hop(offset) * 2 + core))
+    each_chip(lambda there: push(w_ag.at[chip], w_ag.at[chip], 3, (z, there)), False)
 
     exchange(send_b, recv_b, sendx_b, recvx_b, 4)
     store(master, master_out, 0)

time: 51.9 us -> 49.1 us (0.946)
  Pallas kernels: 51.1 us -> 48.3 us
    pallas_call x1, Pallas kernels: 49.1 us -> 46.3 us  [body(): pl.pallas_call(functools.partial(kernel, sizes, scale), out_shape=landed,...]
where the time goes in v4:
time: 49.1 us; the launch traced here: 48.9 us
  Pallas kernels  48.3 us (98%)
  between operations  0.64 us (1%)
    pallas_call x1, Pallas kernels, body(): pl.pallas_call(functools.partial(kernel, sizes, scale), out_shape=landed,...  46.3 us
    pallas_call x1, Pallas kernels, body(): pl.pallas_call(functools.partial(finish, nz), out_shape=outs, in_specs=[h...  2.02 us

profile of v4, /device:TPU:1, one launch (start us, length us, event | category | flops | bytes accessed | tf_op | source)
XLA Modules:
  0.0 48.9 jit_solution(297840311215684231)
XLA Ops:
  0.6 46.3 %shard_map.131 = (bf16[512,256]{1,0:T(8,128)(2,1)}, bf16[64,16,128]{2,1,0:T(8,128)(2,1)}, bf16[12,16,128]{2,1,0:T(8,128)(2,1)}, bf16[2,32,16,128]{3,2,1,0:T(8,128)(2,1)}) custom-call(bf16[1152,256]{1,0:T(8,128)(2,1)} %cot_hbm.1, bf16[512,256]{1,0:T(8,128)(2,1)} %feat_hbm.1, bf16[512,256]{1,0:T(8,128)(2,1)} %agg_hbm.1, bf16[256,256]{1,0:T(8,128)(2,1)} %wself_hbm.1, ...), custom_call_target="tpu_custom_call" | custom-call | tf_op jit(solution)/shard_map/pallas_call | solution.py:376
  46.9 2.0 %shard_map.132 = (bf16[1152,256]{1,0:T(8,128)(2,1)}, f32[2,256,256]{2,1,0:T(8,128)}) custom-call(bf16[512,256]{1,0:T(8,128)(2,1)} %get-tuple-element.6.master_in, bf16[64,16,128]{2,1,0:T(8,128)(2,1)} %get-tuple-element.7.recv_in, bf16[12,16,128]{2,1,0:T(8,128)(2,1)} %get-tuple-element.8.recvx_in, bf16[2,32,16,128]{3,2,1,0:T(8,128)(2,1)} %get-tuple-element.9.w_in), custom_call_target="tpu_custom_call" | custom-call | tf_op jit(solution)/shard_map/pallas_call | solution.py:426

commit v5 on v4

--- a/solution.py
+++ b/solution.py
@@ -125,17 +125,19 @@
 
     each_z(lambda there: greet((there, d)))
 
-    loads = []
-    for place, (src, dst) in enumerate(
-        [(cot_hbm, cot), (wneigh_hbm, wneigh), (trow_hbm, trow), (tcol_hbm, tcol),
-         (tiles_hbm, tiles), (feat_hbm, feat), (agg_hbm, agg), (wself_hbm, wself),
-         (mrow_hbm, mrow), (mcnt_hbm, mcnt), (xrow_hbm, xrow), (xcnt_hbm, xcnt)]
-    ):
-        load = pltpu.make_async_copy(src, dst, load_sem.at[place])
+    loads = [
+        pltpu.make_async_copy(src, dst, load_sem.at[place])
+        for place, (src, dst) in enumerate(
+            [(cot_hbm, cot), (wneigh_hbm, wneigh), (trow_hbm, trow), (tcol_hbm, tcol),
+             (tiles_hbm, tiles), (feat_hbm, feat), (agg_hbm, agg), (wself_hbm, wself),
+             (mrow_hbm, mrow), (mcnt_hbm, mcnt), (xrow_hbm, xrow), (xcnt_hbm, xcnt)]
+        )
+    ]
+    for load in loads[:2]:
         load.start()
-        loads.append(load)
-
     each_chip(lambda there: greet((z, there)), True)
+    for load in loads[2:]:
+        load.start()
 
     def push(src, dst, stage, target):
         copy = pltpu.make_async_remote_copy(

time: 49.1 us -> 48.5 us (0.988)
  Pallas kernels: 48.3 us -> 47.7 us
    pallas_call x1, Pallas kernels: 46.3 us -> 45.7 us  [body(): pl.pallas_call(functools.partial(kernel, sizes, scale), out_shape=landed,...]
where the time goes in v5:
time: 48.5 us; the launch traced here: 48.3 us
  Pallas kernels  47.7 us (98%)
  between operations  0.64 us (1%)
    pallas_call x1, Pallas kernels, body(): pl.pallas_call(functools.partial(kernel, sizes, scale), out_shape=landed,...  45.7 us
    pallas_call x1, Pallas kernels, body(): pl.pallas_call(functools.partial(finish, nz), out_shape=outs, in_specs=[h...  2.02 us

profile of v5, /device:TPU:1, one launch (start us, length us, event | category | flops | bytes accessed | tf_op | source)
XLA Modules:
  0.0 48.3 jit_solution(2451397056635360444)
XLA Ops:
  0.6 45.7 %shard_map.131 = (bf16[512,256]{1,0:T(8,128)(2,1)}, bf16[64,16,128]{2,1,0:T(8,128)(2,1)}, bf16[12,16,128]{2,1,0:T(8,128)(2,1)}, bf16[2,32,16,128]{3,2,1,0:T(8,128)(2,1)}) custom-call(bf16[1152,256]{1,0:T(8,128)(2,1)} %cot_hbm.1, bf16[512,256]{1,0:T(8,128)(2,1)} %feat_hbm.1, bf16[512,256]{1,0:T(8,128)(2,1)} %agg_hbm.1, bf16[256,256]{1,0:T(8,128)(2,1)} %wself_hbm.1, ...), custom_call_target="tpu_custom_call" | custom-call | tf_op jit(solution)/shard_map/pallas_call | solution.py:378
  46.3 2.0 %shard_map.132 = (bf16[1152,256]{1,0:T(8,128)(2,1)}, f32[2,256,256]{2,1,0:T(8,128)}) custom-call(bf16[512,256]{1,0:T(8,128)(2,1)} %get-tuple-element.6.master_in, bf16[64,16,128]{2,1,0:T(8,128)(2,1)} %get-tuple-element.7.recv_in, bf16[12,16,128]{2,1,0:T(8,128)(2,1)} %get-tuple-element.8.recvx_in, bf16[2,32,16,128]{3,2,1,0:T(8,128)(2,1)} %get-tuple-element.9.w_in), custom_call_target="tpu_custom_call" | custom-call | tf_op jit(solution)/shard_map/pallas_call | solution.py:428
